TPU v7x, 512 devices: a whole 4x8x8 slice. The times are simulated.
512 devices in a mesh: expert: 16 (over x, z_hi, core), shard: 8 (over y), replica: 4 (over z_lo).
Axes of the slice: x: 4, y: 8, z: 8 (z_hi: 2, z_lo: 4; z = z_hi * 4 + z_lo), core: 2. Of those that a mesh axis runs over, the one named last changes fastest.
Arguments:
- grad_out: bfloat16 [1024, 3072], P('expert'), may hold values from -6 to 6
- gate_probs: bfloat16 [1024, 4], P('expert'), may hold values from 0.049804688 to 1
- expert_ids: int32 [1024, 4], P('expert'), may hold values from 0 to 15, all different within a row; in each aligned block of 64 rows (0 to 63, 64 to 127, ...) at most 32 rows name the same one
- saved_hidden: bfloat16 [16, 5376, 512], P('expert', ('shard', 'replica')), may hold values from -6 to 6
- down_weight: bfloat16 [16, 5376, 3072], P('expert', ('shard', 'replica')), may hold values from -0.078125 to 0.078125
Outputs:
- grad_hidden: bfloat16 [16, 5376, 512], P('expert', ('shard', 'replica'))
- grad_down: bfloat16 [16, 5376, 3072], P('expert', ('shard', 'replica'))
- grad_gates: float32 [1024, 4], P('expert')
Inputs may be any that keep to these rules, and one draw needn't show every extreme that they name: `expert_ids`: each row names 4 different experts. In each aligned block of 64 rows, no expert is named by more than 32 rows, a bound that some block reaches.
All inputs are finite; a program needn't handle non-finite values.
Results may differ from a plain program's by a relative error of at most 0.0049.
Values may be sent and summed in bfloat16 or wider, within the bound.
A program may use at most 64 MiB of HBM per device.

v0:
```python
import jax
import jax.numpy as jnp
from jax import lax
from jax.sharding import PartitionSpec as P


def assign_positions(ids_flat, experts):
    onehot = (ids_flat[..., None] == lax.broadcasted_iota(jnp.int32, (1, experts), 1)).astype(
        jnp.int32
    )
    before = jnp.cumsum(onehot, axis=-2) - onehot
    return jnp.sum(before * onehot, axis=-1)


def slot_sources(slot_index, slot_count):
    matched = slot_index[None, :] == lax.broadcasted_iota(jnp.int32, (slot_count, 1), 0)
    order_idx = lax.broadcasted_iota(jnp.int32, (1, slot_index.shape[0]), 1)
    source = jnp.sum(jnp.where(matched, order_idx, 0), axis=1)
    filled = jnp.any(matched, axis=1)
    return (source, filled)


def fill_slots(token_rows, token_probs, source, filled, top_k):
    token_idx = source // top_k
    dy_rows = jnp.where(filled[:, None], token_rows[token_idx], jnp.zeros((), token_rows.dtype))
    prob_rows = jnp.where(filled, token_probs.reshape(-1)[source].astype(jnp.float32), 0.0)
    grad_rows = (prob_rows[:, None] * dy_rows.astype(jnp.float32)).astype(jnp.bfloat16)
    return (grad_rows, dy_rows)


def shards(grad_out, gate_probs, expert_ids, saved_hidden, down_weight):
    experts = lax.axis_size("expert")
    local_tokens, top_k = expert_ids.shape
    width = grad_out.shape[1]
    capacity = min(local_tokens, 2 * local_tokens * top_k // experts)
    slot_count = experts * capacity
    own_ids = expert_ids.reshape(-1)
    own_slot = own_ids * capacity + assign_positions(own_ids, experts)
    source, filled = slot_sources(own_slot, slot_count)
    grad_send, dy_send = fill_slots(grad_out, gate_probs, source, filled, top_k)
    grad_slots, dy_slots = (
        lax.all_to_all(
            grad_send.reshape(experts, capacity, width),
            "expert",
            split_axis=0,
            concat_axis=0,
            tiled=True,
        ),
        lax.all_to_all(
            dy_send.reshape(experts, capacity, width),
            "expert",
            split_axis=0,
            concat_axis=0,
            tiled=True,
        ),
    )
    grad_slots = grad_slots.reshape(slot_count, width)
    dy_slots = dy_slots.reshape(slot_count, width)
    hidden = saved_hidden[0]
    weight = down_weight[0]
    grad_hid = lax.dot_general(
        weight, grad_slots, (((1,), (1,)), ((), ())), preferred_element_type=jnp.float32
    ).astype(jnp.bfloat16)
    grad_weight = jnp.dot(hidden, grad_slots, preferred_element_type=jnp.float32).astype(
        jnp.bfloat16
    )
    projected = lax.dot_general(
        weight, dy_slots, (((1,), (1,)), ((), ())), preferred_element_type=jnp.float32
    )
    partial_scores = jnp.sum(hidden.astype(jnp.float32) * projected, axis=0)
    row_scores = lax.psum(partial_scores, ("shard", "replica"))
    returned = lax.all_to_all(
        row_scores.reshape(experts, capacity), "expert", split_axis=0, concat_axis=0, tiled=True
    )
    grad_gates = returned.reshape(-1)[own_slot].reshape(local_tokens, top_k)
    return (grad_hid[None], grad_weight[None], grad_gates)


def solution(mesh):
    in_specs = (
        P("expert", None),
        P("expert", None),
        P("expert", None),
        P("expert", ("shard", "replica"), None),
        P("expert", ("shard", "replica"), None),
    )
    out_specs = (
        P("expert", ("shard", "replica"), None),
        P("expert", ("shard", "replica"), None),
        P("expert", None),
    )
    return jax.shard_map(shards, mesh=mesh, in_specs=in_specs, out_specs=out_specs, check_vma=False)
```

profile of v0, /device:TPU:1, one launch (start us, length us, event | category | flops | bytes accessed | tf_op | source)
XLA Modules:
  0.0 275.7 jit_solution(3932925100057761344)
XLA Ops:
  0.7 0.9 copy.14
  1.6 0.1 reshape.179
  1.8 0.6 reduce-window.6
  2.4 0.2 slice_reduce_fusion
  2.7 0.2 select_reduce_fusion
  2.8 0.2 fusion.6
  3.0 0.8 copy.17
  3.8 0.1 reshape.181
  3.9 3.4 %gather_fusion = bf16[512]{0:T(512)(128)(2,1)S(1)} fusion(bf16[256]{0:T(256)(128)(2,1)S(1)} %reshape.181, s32[1024]{0:T(1024)S(1)} %pad_clamp_fusion.2), kind=kCustom, calls=%fused_computation | custom fusion | bytes 4096 | tf_op jit(solution)/shard_map/gather | solution.py:26
  7.5 3.9 %gather_fusion.1 = bf16[512,3072]{1,0:T(8,128)(2,1)} fusion(bf16[64,3072]{1,0:T(8,128)(2,1)S(1)} %copy-done.1, s32[1024]{0:T(1024)S(1)} %pad_clamp_fusion.1), kind=kCustom, calls=%fused_computation.1 | custom fusion | bytes 6293504 | tf_op jit(solution)/shard_map/gather | solution.py:25
  11.4 5.6 %multiply_convert_fusion = (bf16[16,32,3072]{2,1,0:T(8,128)(2,1)}, bf16[16,32,3072]{2,1,0:T(8,128)(2,1)S(1)}) fusion(f32[16,32]{1,0:T(8,128)S(1)} %broadcast_select_fusion.1, bf16[16,32,3072]{2,1,0:T(8,128)(2,1)} %bitcast.53, pred[16,32]{1,0:T(8,128)(4,1)S(1)} %reduce_or.12), kind=kLoop, calls=%fused_computation.3 | loop fusion | flops 6291456 | bytes 9439744 | tf_op jit(solution)/shard_map/convert_element_type | solution.py:27
  16.9 56.3 %all_to_all.19 = bf16[16,32,3072]{2,1,0:T(8,128)(2,1)} all-to-all(bf16[16,32,3072]{2,1,0:T(8,128)(2,1)S(1)} %get-tuple-element.10), channel_id=1, replica_groups=mesh['expert'=16,'shard'=8,'replica'=4] {'expert'}, dimensions={0} | all-to-all | bytes 6291456 | tf_op jit(solution)/shard_map/all_to_all | solution.py:49
  73.3 35.2 %all-to-all-start = ((bf16[16,32,3072]{2,1,0:T(8,128)(2,1)}), bf16[16,32,3072]{2,1,0:T(8,128)(2,1)}, u32[]{:S(2)}, u32[]{:S(2)}) async-start(bf16[16,32,3072]{2,1,0:T(8,128)(2,1)} %get-tuple-element.9), calls=%async_computation | async-start | bytes 6291456 | tf_op jit(solution)/shard_map/all_to_all | solution.py:42
  108.6 0.1 mul.47
  108.8 3.1 %fusion.2 = f32[512]{0:T(512)S(1)} fusion(bf16[512,3072]{1,0:T(8,128)(2,1)} %bitcast.54, bf16[1,168,3072]{2,1,0:T(8,128)(2,1)S(1)} %copy-done, bf16[1,168,512]{2,1,0:T(8,128)(2,1)S(1)} %copy-done.2), kind=kOutput, calls=%fused_computation.10 | convolution fusion | flops 528739840 | bytes 4352000 | tf_op jit(solution)/shard_map/dot_general | solution.py:67
  112.0 129.0 %psum.7 = f32[16,1,32]{2,1,0:T(1,128)} all-reduce(f32[16,1,32]{2,1,0:T(1,128)S(1)} %all_to_all.14), channel_id=1, replica_groups=mesh['expert'=16,'shard'=8,'replica'=4] {'shard','replica'}, use_global_device_ids=true, to_apply=%region_6.7 | all-reduce | flops 512 | bytes 4096 | tf_op jit(solution)/shard_map/psum | solution.py:71
  241.0 21.4 %all-to-all-start.2 = ((f32[16,1,32]{2,1,0:T(1,128)}), f32[16,1,32]{2,1,0:T(1,128)S(1)}, u32[]{:S(2)}, u32[]{:S(2)}) async-start(f32[16,1,32]{2,1,0:T(1,128)} %psum.7), calls=%async_computation.2 | async-start | bytes 16384 | tf_op jit(solution)/shard_map/all_to_all | solution.py:72
  262.4 3.8 %fusion.3 = bf16[1,168,512]{2,1,0:T(8,128)(2,1)} fusion(bf16[512,3072]{1,0:T(8,128)(2,1)} %bitcast.5, bf16[1,168,3072]{2,1,0:T(8,128)(2,1)S(1)} %copy-done), kind=kOutput, calls=%fused_computation.11 | convolution fusion | flops 528568320 | bytes 4349952 | tf_op jit(solution)/shard_map/dot_general | solution.py:61
  266.1 3.6 %fusion = bf16[1,168,3072]{2,1,0:T(8,128)(2,1)} fusion(bf16[512,3072]{1,0:T(8,128)(2,1)} %bitcast.5, bf16[1,168,512]{2,1,0:T(8,128)(2,1)S(1)} %copy-done.2), kind=kOutput, calls=%fused_computation.5 | convolution fusion | flops 528998400 | bytes 4349952 | tf_op jit(solution)/shard_map/dot_general | solution.py:64
  269.7 2.1 all-to-all-done.2
  271.8 0.5 broadcast.152
  272.3 0.7 reduce.5
  273.0 1.9 gather_fusion.2
  275.1 0.7 copy.19
  (28 shorter events, 0.8 us)
Async XLA Ops:
  0.6 108.1 %copy-start = (bf16[1,168,3072]{2,1,0:T(8,128)(2,1)S(1)}, bf16[1,168,3072]{2,1,0:T(8,128)(2,1)}, u32[]{:S(2)}) copy-start(bf16[1,168,3072]{2,1,0:T(8,128)(2,1)} %param.9) | copy-start | bytes 3096580
  0.6 6.9 %copy-start.1 = (bf16[64,3072]{1,0:T(8,128)(2,1)S(1)}, bf16[64,3072]{1,0:T(8,128)(2,1)}, u32[]{:S(2)}) copy-start(bf16[64,3072]{1,0:T(8,128)(2,1)} %param.5) | copy-start | bytes 1179652
  73.3 35.2 %copy-start.3 = (s32[64,4]{0,1:T(4,128)S(1)}, s32[64,4]{0,1:T(4,128)}, u32[]{:S(2)}) copy-start(s32[64,4]{0,1:T(4,128)} %param.7) | copy-start | bytes 3076
  73.3 35.5 %copy-start.2 = (bf16[1,168,512]{2,1,0:T(8,128)(2,1)S(1)}, bf16[1,168,512]{2,1,0:T(8,128)(2,1)}, u32[]{:S(2)}) copy-start(bf16[1,168,512]{2,1,0:T(8,128)(2,1)} %param.8) | copy-start | bytes 516100
  73.3 167.7 %all-to-all-start = ((bf16[16,32,3072]{2,1,0:T(8,128)(2,1)}), bf16[16,32,3072]{2,1,0:T(8,128)(2,1)}, u32[]{:S(2)}, u32[]{:S(2)}) async-start(bf16[16,32,3072]{2,1,0:T(8,128)(2,1)} %get-tuple-element.9), calls=%async_computation | async-start | bytes 6291456 | tf_op jit(solution)/shard_map/all_to_all | solution.py:42
  241.0 30.8 %all-to-all-start.2 = ((f32[16,1,32]{2,1,0:T(1,128)}), f32[16,1,32]{2,1,0:T(1,128)S(1)}, u32[]{:S(2)}, u32[]{:S(2)}) async-start(f32[16,1,32]{2,1,0:T(1,128)} %psum.7), calls=%async_computation.2 | async-start | bytes 16384 | tf_op jit(solution)/shard_map/all_to_all | solution.py:72
where the time goes:
time: 276 us
  blocking collectives  185 us (67%)
  starting transfers between devices  56.6 us (21%)
  local copies, waits for them, and re-layouts  13.2 us (5%)
  matrix products  10.4 us (4%)
  other arithmetic  7.36 us (3%)
    psum x1, blocking collectives, shards(): row_scores = lax.psum(partial_scores, ('shard', 'replica'))  129 us
    all_to_all x1, blocking collectives, shards(): lax.all_to_all(dy_send.reshape(experts, capacity, width), 'expert', split...  56.3 us
    all_to_all x1, starting transfers between devices, shards(): lax.all_to_all(grad_send.reshape(experts, capacity, width), 'expert', spl...  35.2 us
    all_to_all x1, starting transfers between devices, shards(): lax.all_to_all(row_scores.reshape(experts, capacity), 'expert', split_axi...  21.4 us
    convert_element_type x1, other arithmetic, fill_slots(): (prob_rows[:, None] * dy_rows.astype(jnp.float32)).astype(jnp.bfloat16)  5.59 us
  transfers between devices with their start and end apart: 2, of which 1 were waited for; matrix products, arithmetic and copies ran while one was open for 4% of the time, Pallas kernels for 0%

commit v1 on v0

v1 whole, which is shorter than its diff:
```python
import functools

import jax
import jax.numpy as jnp
from jax import lax
from jax.experimental import pallas as pl
from jax.experimental.pallas import tpu as pltpu
from jax.sharding import PartitionSpec as P

MESH = pl.DeviceIdType.MESH
NX, NY, NR = 4, 8, 4
NE = 16
TOK, TOP, CAP = 64, 4, 32
CH = 16
ORDER = (0, 1, 3, 2)
PLANE = NY * NR
F32, BF16 = jnp.float32, jnp.bfloat16


def kernel(
    ids_ref, gates_ref, tok_hbm, hid_hbm, w_hbm,
    gh_hbm, gd_hbm, score_ref,
    rows, w, hid, spread, gh, gd, before, meta, part, sc1, sc2,
    load_sem, out_sem, ss, rs, ds, rd, meta_s, meta_r, s1_s, s1_r, s2_s, s2_r,
):
    e, y, r = lax.axis_index("expert"), lax.axis_index("shard"), lax.axis_index("replica")
    x, half, core = e // 4, (e // 2) % 2, e % 2
    plane = y * NR + r
    cls = (y + 2 * r) % 4

    def expert(xx, hh, cc):
        return xx * 4 + hh * 2 + cc

    x1 = (expert((x + 1) % NX, half, core), y, r)
    x3 = (expert((x + 3) % NX, half, core), y, r)
    x2 = (expert((x + 2) % NX, half, core), y, r)
    y1, y7 = (e, (y + 1) % NY, r), (e, (y + 7) % NY, r)
    zn = (e, y, r + 1 - 2 * (r % 2))
    mirror = (expert(x, 1 - half, core), y, NR - 1 - r)
    twin = (expert(x, half, 1 - core), y, r)

    own_row = pl.multiple_of(e * TOK, TOK)
    load_tok = pltpu.make_async_copy(tok_hbm, rows.at[pl.ds(own_row, TOK)], load_sem.at[0])
    load_w = pltpu.make_async_copy(w_hbm, w, load_sem.at[1])
    load_h = pltpu.make_async_copy(hid_hbm, hid, load_sem.at[2])
    load_tok.start()

    barrier = pltpu.get_barrier_semaphore()
    for k in range(1, NE):
        pl.semaphore_signal(barrier, inc=1, device_id=((e + k) % NE, y, r), device_id_type=MESH)

    def greet(k, _):
        p = (plane + k) % PLANE
        pl.semaphore_signal(barrier, inc=1, device_id=(e, p // NR, p % NR), device_id_type=MESH)
        return 0

    lax.fori_loop(1, PLANE, greet, 0)
    pl.semaphore_signal(barrier, inc=1, device_id=mirror, device_id_type=MESH)
    load_w.start()
    load_h.start()

    place = (
        lax.broadcasted_iota(jnp.int32, (TOK, 128), 1)
        == lax.broadcasted_iota(jnp.int32, (TOK, 128), 0) + TOK * core
    ).astype(F32).astype(BF16)
    turned = (((0,), (0,)), ((), ()))
    meta[e, 0:4, :] = lax.dot_general(ids_ref[...].astype(F32).astype(BF16), place, turned, preferred_element_type=F32)
    meta[e, 4:8, :] = lax.dot_general(gates_ref[...], place, turned, preferred_element_type=F32)
    t_from = lax.broadcasted_iota(jnp.int32, (256, 256), 0)
    t_to = lax.broadcasted_iota(jnp.int32, (256, 256), 1)
    before[...] = ((t_from < t_to) & (t_from // TOK == t_to // TOK)).astype(F32).astype(BF16)

    pl.semaphore_wait(barrier, NE - 1 + PLANE - 1 + 1)

    sent, shared = [], []

    def block_row(h, dx, cc, k):
        b = expert((x + dx) % NX, half if h == 0 else 1 - half, cc)
        return pl.multiple_of(b * TOK + k * CH, CH)

    def arrival(h, dx, k):
        ref = rows.at[pl.ds(block_row(h, dx, core, k), CH)]
        return pltpu.make_async_remote_copy(
            src_ref=ref, dst_ref=ref, send_sem=ss.at[0], recv_sem=rs.at[h * 4 + dx, k], device_id=x1, device_id_type=MESH
        )

    def from_twin(h, dx, k):
        ref = rows.at[pl.ds(block_row(h, dx, 1 - core, k), CH)]
        return pltpu.make_async_remote_copy(
            src_ref=ref, dst_ref=ref, send_sem=ss.at[0], recv_sem=rd.at[h * 4 + dx, k], device_id=twin, device_id_type=MESH
        )

    def send(h, dx, k, to, there_h, there_dx):
        ref = rows.at[pl.ds(block_row(h, dx, core, k), CH)]
        copy = pltpu.make_async_remote_copy(
            src_ref=ref, dst_ref=ref, send_sem=ss.at[len(sent)], recv_sem=rs.at[there_h * 4 + there_dx, k],
            device_id=to, device_id_type=MESH,
        )
        copy.start()
        sent.append(copy)

    def share(h, dx, k):
        ref = rows.at[pl.ds(block_row(h, dx, core, k), CH)]
        copy = pltpu.make_async_remote_copy(
            src_ref=ref, dst_ref=ref, send_sem=ds.at[h * 4 + dx, k], recv_sem=rd.at[h * 4 + dx, k],
            device_id=twin, device_id_type=MESH,
        )
        copy.start()
        shared.append(copy)

    k0, k1, k2, k3 = cls, (cls + 1) % 4, (cls + 2) % 4, (cls + 3) % 4

    load_tok.wait()
    send(0, 0, k2, mirror, 1, 0)
    for to, dx in ((x1, 3), (x3, 1), (x2, 2)):
        send(0, 0, k0, to, 0, dx)
    for to, dx, kk in ((x1, 3, k2), (x3, 1, k2), (x1, 3, k3), (x3, 1, k1)):
        send(0, 0, kk, to, 0, dx)

    def meta_copy(k):
        other = (e + k) % NE
        return pltpu.make_async_remote_copy(
            src_ref=meta.at[e], dst_ref=meta.at[e], send_sem=meta_s.at[k], recv_sem=meta_r.at[e],
            device_id=(other, y, r), device_id_type=MESH,
        )

    for k in range(1, NE):
        meta_copy(k).start()
    for k in range(4):
        share(0, 0, k)

    arrival(1, 0, k0).wait_recv()
    for to, dx in ((x1, 3), (x3, 1), (x2, 2)):
        send(1, 0, k0, to, 1, dx)
    for to in (y1, y7, zn):
        send(1, 0, k0, to, 1, 0)
    share(1, 0, k0)
    arrival(0, 1, k0).wait_recv()
    send(0, 1, k0, y1, 0, 1)
    share(0, 1, k0)
    arrival(0, 3, k0).wait_recv()
    send(0, 3, k0, y7, 0, 3)
    share(0, 3, k0)
    arrival(0, 2, k0).wait_recv()
    for to in (y1, y7, zn):
        send(0, 2, k0, to, 0, 2)
    share(0, 2, k0)
    for dx in (1, 3, 2):
        arrival(1, dx, k0).wait_recv()
        for to in (y1, y7, zn):
            send(1, dx, k0, to, 1, dx)
        share(1, dx, k0)

    def take(h, dx, ks):
        for k in ks:
            arrival(h, dx, k).wait_recv()
            share(h, dx, k)

    load_w.wait()
    load_h.wait()
    for k in range(1, NE):
        other = (e + NE - k) % NE
        pltpu.make_async_remote_copy(
            src_ref=meta.at[other], dst_ref=meta.at[other], send_sem=meta_s.at[k], recv_sem=meta_r.at[other],
            device_id=(other, y, r), device_id_type=MESH,
        ).wait_recv()

    by_row = (((1,), (1,)), ((), ()))
    lane_block = lax.broadcasted_iota(jnp.int32, (1, 256), 1) // TOK
    scored = []
    for i, dx in enumerate(ORDER):
        if dx == 0:
            take(1, 0, (k1, k3, k2))
        else:
            take(0, dx, (k2, k1, k3) if dx != 3 else (k2, k3, k1))
            take(1, dx, (k1, k3, k2))
        for k in range(4):
            from_twin(0, dx, k).wait_recv()
            from_twin(1, dx, k).wait_recv()
        g = (x + dx) % NX
        here = pl.ds(pl.multiple_of(g * 256, 256), 256)
        slots = pl.ds(pl.multiple_of(g * 128, 128), 128)
        named = jnp.concatenate([meta[4 * g] + meta[4 * g + 1], meta[4 * g + 2] + meta[4 * g + 3]], axis=1)
        mine = named[0:4] == e.astype(F32)
        took = jnp.sum(mine.astype(F32), axis=0, keepdims=True)
        gate = jnp.sum(jnp.where(mine, named[4:8], 0.0), axis=0, keepdims=True)
        position = jnp.dot(
            jnp.broadcast_to(took, (8, 256)).astype(BF16), before[...], preferred_element_type=F32
        )[0:1]
        slot = jnp.where(took > 0.5, position.astype(jnp.int32) + lane_block * CAP, -1)
        pick = (lax.broadcasted_iota(jnp.int32, (128, 256), 0) == slot).astype(F32).astype(BF16)
        hs = jnp.dot(hid[:, slots], pick, preferred_element_type=F32)
        proj = lax.dot_general(w[...], rows[here, :], by_row, preferred_element_type=F32)
        score = jnp.sum(hs * proj, axis=0, keepdims=True)
        terms = jnp.where(mine, score, 0.0)
        for h in range(2):
            part[i, h, 0:4, :] = terms[:, 128 * h : 128 * h + 128]
            part[i, h, 4:8, :] = jnp.zeros((4, 128), F32)
        for h in range(2):
            for cc in range(2):
                there_h = half if h == 0 else 1 - half
                there_c = core if cc == 0 else 1 - core
                if dx == 0 and h == 0 and cc == 0:
                    continue
                copy = pltpu.make_async_remote_copy(
                    src_ref=part.at[i, there_h], dst_ref=sc1.at[e], send_sem=s1_s.at[i * 4 + h * 2 + cc],
                    recv_sem=s1_r.at[e], device_id=(expert(g, there_h, there_c), y, r), device_id_type=MESH,
                )
                copy.start()
                scored.append(copy)
        if dx == 0:
            sc1[e] = part[i, half]
        spread[:, here] = (hs * gate).astype(BF16)
        gh[:, slots] = lax.dot_general(
            (proj * gate).astype(BF16), pick, by_row, preferred_element_type=F32
        ).astype(BF16)

    out_h = pltpu.make_async_copy(gh, gh_hbm, out_sem.at[0])
    out_h.start()

    for k in range(1, NE):
        other = (e + k) % NE
        pltpu.make_async_remote_copy(
            src_ref=sc1.at[other], dst_ref=sc1.at[other], send_sem=s1_s.at[0], recv_sem=s1_r.at[other],
            device_id=(other, y, r), device_id_type=MESH,
        ).wait_recv()
    sc2[plane] = jnp.sum(sc1[...], axis=0)

    def plane_copy(k, at):
        p = (plane + k) % PLANE
        return pltpu.make_async_remote_copy(
            src_ref=sc2.at[at], dst_ref=sc2.at[at], send_sem=s2_s.at[k], recv_sem=s2_r.at[at],
            device_id=(e, p // NR, p % NR), device_id_type=MESH,
        )

    def tell(k, _):
        plane_copy(k, plane).start()
        return 0

    lax.fori_loop(1, PLANE, tell, 0)

    width = 512

    def weight_columns(j, _):
        cols = pl.ds(pl.multiple_of(j * width, width), width)
        gd[:, cols] = jnp.dot(spread[...], rows[:, cols], preferred_element_type=F32).astype(BF16)
        return 0

    lax.fori_loop(0, gd.shape[1] // width, weight_columns, 0)
    out_d = pltpu.make_async_copy(gd, gd_hbm, out_sem.at[1])
    out_d.start()

    def hear(k, _):
        plane_copy(k, (plane + k) % PLANE).wait_recv()
        return 0

    lax.fori_loop(1, PLANE, hear, 0)
    total = jnp.sum(sc2[...], axis=0)
    score_ref[...] = jnp.where(core == 0, total[:, 0:TOK], total[:, TOK : 2 * TOK])

    def told(k, _):
        plane_copy(k, plane).wait_send()
        return 0

    lax.fori_loop(1, PLANE, told, 0)
    for copy in sent + shared + scored:
        copy.wait_send()
    for k in range(1, NE):
        meta_copy(k).wait_send()
    out_h.wait()
    out_d.wait()


def shards(grad_out, gate_probs, expert_ids, saved_hidden, down_weight):
    hidden, weight = saved_hidden[0], down_weight[0]
    units, slots = hidden.shape
    width = weight.shape[1]
    dma = pltpu.SemaphoreType.DMA
    anywhere = pl.BlockSpec(memory_space=pl.ANY)
    vmem = pl.BlockSpec(memory_space=pltpu.VMEM)
    gh, gd, scores = pl.pallas_call(
        kernel,
        out_shape=(
            jax.ShapeDtypeStruct((units, slots), BF16),
            jax.ShapeDtypeStruct((units, width), BF16),
            jax.ShapeDtypeStruct((8, TOK), F32),
        ),
        in_specs=[vmem, vmem, anywhere, anywhere, anywhere],
        out_specs=(anywhere, anywhere, vmem),
        scratch_shapes=[
            pltpu.VMEM((NE * TOK, width), BF16),
            pltpu.VMEM((units, width), BF16),
            pltpu.VMEM((units, slots), BF16),
            pltpu.VMEM((units, NE * TOK), BF16),
            pltpu.VMEM((units, slots), BF16),
            pltpu.VMEM((units, width), BF16),
            pltpu.VMEM((256, 256), BF16),
            pltpu.VMEM((NE, 8, 128), F32),
            pltpu.VMEM((NX, 2, 8, 128), F32),
            pltpu.VMEM((NE, 8, 128), F32),
            pltpu.VMEM((PLANE, 8, 128), F32),
            dma((3,)),
            dma((2,)),
            dma((28,)),
            dma((8, 4)),
            dma((8, 4)),
            dma((8, 4)),
            dma((NE,)),
            dma((NE,)),
            dma((NE,)),
            dma((NE,)),
            dma((PLANE,)),
            dma((PLANE,)),
        ],
        compiler_params=pltpu.CompilerParams(collective_id=0, has_side_effects=True, vmem_limit_bytes=40 * 2**20),
        cost_estimate=pl.CostEstimate(
            flops=4 * units * width * NE * TOK, bytes_accessed=4 * units * width, transcendentals=0
        ),
    )(expert_ids, gate_probs, grad_out, hidden, weight)
    return gh[None], gd[None], scores[:TOP].T


def solution(mesh):
    split = P("expert", ("shard", "replica"), None)
    rows = P("expert", None)
    return jax.shard_map(
        shards, mesh=mesh, in_specs=(rows, rows, rows, split, split), out_specs=(split, split, rows), check_vma=False
    )
```

time: 276 us -> 65.6 us (0.24)
  blocking collectives: 185 us -> 0 us
  Pallas kernels: 0 us -> 57.9 us
  starting transfers between devices: 56.6 us -> 0 us
  matrix products: 10.4 us -> 0 us
  other arithmetic: 7.36 us -> 0 us
  local copies, waits for them, and re-layouts: 13.2 us -> 6.79 us
    psum x1 -> x0, blocking collectives: 129 us -> none  [shards(): row_scores = lax.psum(partial_scores, ('shard', 'replica'))]
    pallas_call x0 -> x1, Pallas kernels: none -> 57.9 us  [shards(): pl.pallas_call(kernel, out_shape=(jax.ShapeDtypeStruct((units, slots), BF...]
    all_to_all x2 -> x0, starting transfers between devices: 56.6 us -> none  [the longest x1 35.2 us: shards(): lax.all_to_all(grad_send.reshape(experts, capacity, width), 'expert', spl...]
    all_to_all x1 -> x0, blocking collectives: 56.3 us -> none  [shards(): lax.all_to_all(dy_send.reshape(experts, capacity, width), 'expert', split...]
    dot_general x3 -> x0, matrix products: 10.4 us -> none  [the longest x1 3.75 us: shards(): lax.dot_general(weight, grad_slots, (((1,), (1,)), ((), ())), preferred_e...]
    gather x3 -> x0, local copies, waits for them, and re-layouts: 9.16 us -> none  [the longest x1 3.85 us: fill_slots(): token_rows[token_idx]]
    convert_element_type x2 -> x0, other arithmetic: 5.59 us -> none  [the longest x1 5.59 us: fill_slots(): (prob_rows[:, None] * dy_rows.astype(jnp.float32)).astype(jnp.bfloat16)]
    unnamed x11 -> x14, local copies, waits for them, and re-layouts: 2.34 us -> 6.21 us
  transfers between devices with their start and end apart: 2 -> 0, of which waited for: 1 -> 0; matrix products, arithmetic and copies ran while one was open for 4% -> 0% of each run, Pallas kernels for 0% -> 0%
where the time goes in v1:
time: 65.6 us; the launch traced here: 65.3 us
  Pallas kernels  57.9 us (88%)
  local copies, waits for them, and re-layouts  6.79 us (10%)
    pallas_call x1, Pallas kernels, shards(): pl.pallas_call(kernel, out_shape=(jax.ShapeDtypeStruct((units, slots), BF...  57.9 us
    unnamed x14, local copies, waits for them, and re-layouts  6.21 us

profile of v1, /device:TPU:1, one launch (start us, length us, event | category | flops | bytes accessed | tf_op | source)
XLA Modules:
  0.0 65.3 jit_solution(14109724071059543388)
XLA Ops:
  0.6 0.0 copy-start.4
  0.6 0.7 %copy-done.4 = bf16[64,4]{0,1:T(4,128)(2,1)S(1)} copy-done((bf16[64,4]{0,1:T(4,128)(2,1)S(1)}, bf16[64,4]{0,1:T(4,128)(2,1)}, u32[]{:S(2)}) %copy-start.4) | copy-done | bytes 536
  1.3 0.0 copy-start.3
  1.3 0.1 copy.9.gates_ref
  1.4 0.6 copy-done.3
  2.0 0.1 copy.8.ids_ref
  2.1 0.0 copy-start
  2.1 1.2 %copy-done = bf16[1,168,3072]{2,1,0:T(8,128)(2,1)S(1)} copy-done((bf16[1,168,3072]{2,1,0:T(8,128)(2,1)S(1)}, bf16[1,168,3072]{2,1,0:T(8,128)(2,1)}, u32[]{:S(2)}) %copy-start) | copy-done | bytes 1032216
  3.3 0.0 copy-start.1
  3.3 1.0 %copy-done.1 = bf16[64,3072]{1,0:T(8,128)(2,1)S(1)} copy-done((bf16[64,3072]{1,0:T(8,128)(2,1)S(1)}, bf16[64,3072]{1,0:T(8,128)(2,1)}, u32[]{:S(2)}) %copy-start.1) | copy-done | bytes 393240
  4.3 0.0 copy-start.2
  4.3 0.9 %copy-done.2 = bf16[1,168,512]{2,1,0:T(8,128)(2,1)S(1)} copy-done((bf16[1,168,512]{2,1,0:T(8,128)(2,1)S(1)}, bf16[1,168,512]{2,1,0:T(8,128)(2,1)}, u32[]{:S(2)}) %copy-start.2) | copy-done | bytes 172056
  5.2 57.9 %shard_map.76 = (bf16[168,512]{1,0:T(8,128)(2,1)S(1)}, bf16[168,3072]{1,0:T(8,128)(2,1)S(1)}, f32[8,64]{1,0:T(8,128)S(1)}) custom-call(s32[64,4]{1,0:T(8,128)S(1)} %copy.8.ids_ref, bf16[64,4]{1,0:T(8,128)(2,1)S(1)} %copy.9.gates_ref, bf16[64,3072]{1,0:T(8,128)(2,1)S(1)} %copy-done.1, bf16[168,512]{1,0:T(8,128)(2,1)S(1)} %bitcast.9, bf16[168,3072]{1,0:T(8,128)(2,1)S(1)} %bitcast.8), custom_call_target="tpu_custom_call" | custom-call | flops 2113929216 | bytes 2064384 | tf_op jit(solution)/shard_map/pallas_call | solution.py:281
  63.1 0.6 slice_bitcast_fusion
  63.7 0.7 %copy.12 = bf16[1,168,512]{2,1,0:T(8,128)(2,1)} copy(bf16[1,168,512]{2,1,0:T(8,128)(2,1)S(1)} %bitcast.7) | data formatting | bytes 344064
  64.3 1.0 %copy.13 = bf16[1,168,3072]{2,1,0:T(8,128)(2,1)} copy(bf16[1,168,3072]{2,1,0:T(8,128)(2,1)S(1)} %bitcast.6) | data formatting | bytes 2064384
Async XLA Ops:
  0.6 0.7 %copy-start.4 = (bf16[64,4]{0,1:T(4,128)(2,1)S(1)}, bf16[64,4]{0,1:T(4,128)(2,1)}, u32[]{:S(2)}) copy-start(bf16[64,4]{0,1:T(4,128)(2,1)} %param.6) | copy-start | bytes 1540
  1.3 0.7 %copy-start.3 = (s32[64,4]{0,1:T(4,128)S(1)}, s32[64,4]{0,1:T(4,128)}, u32[]{:S(2)}) copy-start(s32[64,4]{0,1:T(4,128)} %param.7) | copy-start | bytes 3076
  2.1 1.2 %copy-start = (bf16[1,168,3072]{2,1,0:T(8,128)(2,1)S(1)}, bf16[1,168,3072]{2,1,0:T(8,128)(2,1)}, u32[]{:S(2)}) copy-start(bf16[1,168,3072]{2,1,0:T(8,128)(2,1)} %param.9) | copy-start | bytes 3096580
  3.3 1.0 %copy-start.1 = (bf16[64,3072]{1,0:T(8,128)(2,1)S(1)}, bf16[64,3072]{1,0:T(8,128)(2,1)}, u32[]{:S(2)}) copy-start(bf16[64,3072]{1,0:T(8,128)(2,1)} %tok_hbm.1) | copy-start | bytes 1179652
  4.3 0.9 %copy-start.2 = (bf16[1,168,512]{2,1,0:T(8,128)(2,1)S(1)}, bf16[1,168,512]{2,1,0:T(8,128)(2,1)}, u32[]{:S(2)}) copy-start(bf16[1,168,512]{2,1,0:T(8,128)(2,1)} %param.8) | copy-start | bytes 516100

commit v2 on v1

--- a/solution.py
+++ b/solution.py
@@ -18,10 +18,10 @@
 
 
 def kernel(
-    ids_ref, gates_ref, tok_hbm, hid_hbm, w_hbm,
+    ids_hbm, gates_hbm, tok_hbm, hid_hbm, w_hbm,
     gh_hbm, gd_hbm, score_ref,
-    rows, w, hid, spread, gh, gd, before, meta, part, sc1, sc2,
-    load_sem, out_sem, ss, rs, ds, rd, meta_s, meta_r, s1_s, s1_r, s2_s, s2_r,
+    ids, gates, rows, w, hid, spread, gh, gd, before, meta, part, sc1, sc2,
+    load_sem, out_sem, ss, rs, ds, rd, ms, mr, mds, mdr, s1_s, s1_r, s2_s, s2_r, wave, ready,
 ):
     e, y, r = lax.axis_index("expert"), lax.axis_index("shard"), lax.axis_index("replica")
     x, half, core = e // 4, (e // 2) % 2, e % 2
@@ -36,26 +36,28 @@
     x2 = (expert((x + 2) % NX, half, core), y, r)
     y1, y7 = (e, (y + 1) % NY, r), (e, (y + 7) % NY, r)
     zn = (e, y, r + 1 - 2 * (r % 2))
+    far = (e, y, (r + 2) % NR)
     mirror = (expert(x, 1 - half, core), y, NR - 1 - r)
     twin = (expert(x, half, 1 - core), y, r)
+
+    barrier = pltpu.get_barrier_semaphore()
+    near = (x1, x3, x2, y1, y7, zn, far, twin)
+    for other in near:
+        pl.semaphore_signal(barrier, inc=1, device_id=other, device_id_type=MESH)
+
+    @pl.when(half == 0)
+    def _():
+        pl.semaphore_signal(barrier, inc=1, device_id=mirror, device_id_type=MESH)
 
     own_row = pl.multiple_of(e * TOK, TOK)
     load_tok = pltpu.make_async_copy(tok_hbm, rows.at[pl.ds(own_row, TOK)], load_sem.at[0])
     load_w = pltpu.make_async_copy(w_hbm, w, load_sem.at[1])
     load_h = pltpu.make_async_copy(hid_hbm, hid, load_sem.at[2])
+    load_ids = pltpu.make_async_copy(ids_hbm, ids, load_sem.at[3])
+    load_gates = pltpu.make_async_copy(gates_hbm, gates, load_sem.at[4])
     load_tok.start()
-
-    barrier = pltpu.get_barrier_semaphore()
-    for k in range(1, NE):
-        pl.semaphore_signal(barrier, inc=1, device_id=((e + k) % NE, y, r), device_id_type=MESH)
-
-    def greet(k, _):
-        p = (plane + k) % PLANE
-        pl.semaphore_signal(barrier, inc=1, device_id=(e, p // NR, p % NR), device_id_type=MESH)
-        return 0
-
-    lax.fori_loop(1, PLANE, greet, 0)
-    pl.semaphore_signal(barrier, inc=1, device_id=mirror, device_id_type=MESH)
+    load_ids.start()
+    load_gates.start()
     load_w.start()
     load_h.start()
 
@@ -63,14 +65,21 @@
         lax.broadcasted_iota(jnp.int32, (TOK, 128), 1)
         == lax.broadcasted_iota(jnp.int32, (TOK, 128), 0) + TOK * core
     ).astype(F32).astype(BF16)
-    turned = (((0,), (0,)), ((), ()))
-    meta[e, 0:4, :] = lax.dot_general(ids_ref[...].astype(F32).astype(BF16), place, turned, preferred_element_type=F32)
-    meta[e, 4:8, :] = lax.dot_general(gates_ref[...], place, turned, preferred_element_type=F32)
-    t_from = lax.broadcasted_iota(jnp.int32, (256, 256), 0)
-    t_to = lax.broadcasted_iota(jnp.int32, (256, 256), 1)
-    before[...] = ((t_from < t_to) & (t_from // TOK == t_to // TOK)).astype(F32).astype(BF16)
-
-    pl.semaphore_wait(barrier, NE - 1 + PLANE - 1 + 1)
+    load_ids.wait()
+    load_gates.wait()
+    meta[e, 0:4, :] = jnp.dot(ids[...].astype(F32).astype(BF16), place, preferred_element_type=F32)
+    meta[e, 4:8, :] = jnp.dot(gates[...], place, preferred_element_type=F32)
+    pl.semaphore_wait(barrier, len(near) + half)
+
+    @pl.when(half == 1)
+    def _():
+        pl.semaphore_signal(ready, inc=1, device_id=mirror, device_id_type=MESH)
+
+    def ripple(n, *others):
+        for other in others:
+            pl.semaphore_signal(wave.at[n], inc=1, device_id=other, device_id_type=MESH)
+
+    ripple(0, y1, y7)
 
     sent, shared = [], []
 
@@ -108,33 +117,57 @@
         copy.start()
         shared.append(copy)
 
+    def meta_copy(h, dx, to, n, there_h, there_dx, send_sem, recv_sem, cc):
+        ref = meta.at[expert((x + dx) % NX, half if h == 0 else 1 - half, cc)]
+        return pltpu.make_async_remote_copy(
+            src_ref=ref, dst_ref=ref, send_sem=send_sem.at[n], recv_sem=recv_sem.at[there_h * 4 + there_dx],
+            device_id=to, device_id_type=MESH,
+        )
+
+    noted = []
+
+    def note(h, dx, to, there_h, there_dx):
+        copy = meta_copy(h, dx, to, len(noted), there_h, there_dx, ms, mr, core)
+        copy.start()
+        noted.append(copy)
+
+    def note_twin(h, dx):
+        copy = meta_copy(h, dx, twin, h * 4 + dx, h, dx, mds, mdr, core)
+        copy.start()
+        shared.append(copy)
+
+    def noted_here(h, dx):
+        meta_copy(h, dx, twin, 0, h, dx, ms, mr, core).wait_recv()
+        note_twin(h, dx)
+
+    def noted_by_twin(h, dx):
+        meta_copy(h, dx, twin, 0, h, dx, mds, mdr, 1 - core).wait_recv()
+
     k0, k1, k2, k3 = cls, (cls + 1) % 4, (cls + 2) % 4, (cls + 3) % 4
+    along = ((x1, 3), (x3, 1), (x2, 2))
 
     load_tok.wait()
+    for to, dx in along:
+        send(0, 0, k0, to, 0, dx)
+    for to, dx in along:
+        note(0, 0, to, 0, dx)
+
+    @pl.when(half == 0)
+    def _():
+        pl.semaphore_wait(ready, 1)
+
     send(0, 0, k2, mirror, 1, 0)
-    for to, dx in ((x1, 3), (x3, 1), (x2, 2)):
-        send(0, 0, k0, to, 0, dx)
-    for to, dx, kk in ((x1, 3, k2), (x3, 1, k2), (x1, 3, k3), (x3, 1, k1)):
-        send(0, 0, kk, to, 0, dx)
-
-    def meta_copy(k):
-        other = (e + k) % NE
-        return pltpu.make_async_remote_copy(
-            src_ref=meta.at[e], dst_ref=meta.at[e], send_sem=meta_s.at[k], recv_sem=meta_r.at[e],
-            device_id=(other, y, r), device_id_type=MESH,
-        )
-
-    for k in range(1, NE):
-        meta_copy(k).start()
+    note(0, 0, mirror, 1, 0)
+    note_twin(0, 0)
     for k in range(4):
         share(0, 0, k)
-
-    arrival(1, 0, k0).wait_recv()
-    for to, dx in ((x1, 3), (x3, 1), (x2, 2)):
-        send(1, 0, k0, to, 1, dx)
-    for to in (y1, y7, zn):
-        send(1, 0, k0, to, 1, 0)
-    share(1, 0, k0)
+    send(0, 0, k2, x1, 0, 3)
+    send(0, 0, k2, x3, 0, 1)
+
+    t_from = lax.broadcasted_iota(jnp.int32, (256, 256), 0)
+    t_to = lax.broadcasted_iota(jnp.int32, (256, 256), 1)
+    before[...] = ((t_from < t_to) & (t_from // TOK == t_to // TOK)).astype(F32).astype(BF16)
+
     arrival(0, 1, k0).wait_recv()
     send(0, 1, k0, y1, 0, 1)
     share(0, 1, k0)
@@ -146,10 +179,32 @@
         send(0, 2, k0, to, 0, 2)
     share(0, 2, k0)
     for dx in (1, 3, 2):
+        noted_here(0, dx)
+    pl.semaphore_wait(wave.at[0], 2)
+    ripple(1, y1, y7)
+
+    arrival(1, 0, k0).wait_recv()
+    for to, dx in along:
+        send(1, 0, k0, to, 1, dx)
+    for to in (y1, y7, zn):
+        send(1, 0, k0, to, 1, 0)
+    share(1, 0, k0)
+    noted_here(1, 0)
+    for to, dx in along:
+        note(1, 0, to, 1, dx)
+    send(0, 0, k3, x1, 0, 3)
+    send(0, 0, k1, x3, 0, 1)
+    pl.semaphore_wait(wave.at[1], 2)
+    ripple(2, y1, y7)
+    for dx in (1, 3, 2):
         arrival(1, dx, k0).wait_recv()
         for to in (y1, y7, zn):
             send(1, dx, k0, to, 1, dx)
         share(1, dx, k0)
+    for dx in (1, 3, 2):
+        noted_here(1, dx)
+    pl.semaphore_wait(wave.at[2], 2)
+    ripple(3, zn)
 
     def take(h, dx, ks):
         for k in ks:
@@ -158,25 +213,26 @@
 
     load_w.wait()
     load_h.wait()
-    for k in range(1, NE):
-        other = (e + NE - k) % NE
-        pltpu.make_async_remote_copy(
-            src_ref=meta.at[other], dst_ref=meta.at[other], send_sem=meta_s.at[k], recv_sem=meta_r.at[other],
-            device_id=(other, y, r), device_id_type=MESH,
-        ).wait_recv()
+    def bring(dx):
+        take(0, dx, (k2, k1, k3) if dx == 2 else ((k2, k1, k3) if dx == 1 else (k2, k3, k1)))
+        take(1, dx, (k1, k3, k2))
 
     by_row = (((1,), (1,)), ((), ()))
     lane_block = lax.broadcasted_iota(jnp.int32, (1, 256), 1) // TOK
     scored = []
     for i, dx in enumerate(ORDER):
-        if dx == 0:
+        if i == 0:
             take(1, 0, (k1, k3, k2))
-        else:
-            take(0, dx, (k2, k1, k3) if dx != 3 else (k2, k3, k1))
-            take(1, dx, (k1, k3, k2))
+            bring(1)
+            pl.semaphore_wait(wave.at[3], 1)
+            ripple(4, far)
+        elif i < 3:
+            bring(ORDER[i + 1])
         for k in range(4):
             from_twin(0, dx, k).wait_recv()
             from_twin(1, dx, k).wait_recv()
+        noted_by_twin(0, dx)
+        noted_by_twin(1, dx)
         g = (x + dx) % NX
         here = pl.ds(pl.multiple_of(g * 256, 256), 256)
         slots = pl.ds(pl.multiple_of(g * 128, 128), 128)
@@ -204,7 +260,8 @@
                     continue
                 copy = pltpu.make_async_remote_copy(
                     src_ref=part.at[i, there_h], dst_ref=sc1.at[e], send_sem=s1_s.at[i * 4 + h * 2 + cc],
-                    recv_sem=s1_r.at[e], device_id=(expert(g, there_h, there_c), y, r), device_id_type=MESH,
+                    recv_sem=s1_r.at[e], device_id=(expert(g, there_h, there_c), y, r if h == 0 else NR - 1 - r),
+                    device_id_type=MESH,
                 )
                 copy.start()
                 scored.append(copy)
@@ -237,6 +294,7 @@
         plane_copy(k, plane).start()
         return 0
 
+    pl.semaphore_wait(wave.at[4], 1)
     lax.fori_loop(1, PLANE, tell, 0)
 
     width = 512
@@ -256,17 +314,15 @@
 
     lax.fori_loop(1, PLANE, hear, 0)
     total = jnp.sum(sc2[...], axis=0)
-    score_ref[...] = jnp.where(core == 0, total[:, 0:TOK], total[:, TOK : 2 * TOK])
+    score_ref[...] = jnp.where(core == 0, total[0:TOP, 0:TOK], total[0:TOP, TOK : 2 * TOK])
 
     def told(k, _):
         plane_copy(k, plane).wait_send()
         return 0
 
     lax.fori_loop(1, PLANE, told, 0)
-    for copy in sent + shared + scored:
+    for copy in sent + shared + scored + noted:
         copy.wait_send()
-    for k in range(1, NE):
-        meta_copy(k).wait_send()
     out_h.wait()
     out_d.wait()
 
@@ -278,16 +334,19 @@
     dma = pltpu.SemaphoreType.DMA
     anywhere = pl.BlockSpec(memory_space=pl.ANY)
     vmem = pl.BlockSpec(memory_space=pltpu.VMEM)
+    hbm = pl.BlockSpec(memory_space=pltpu.HBM)
     gh, gd, scores = pl.pallas_call(
         kernel,
         out_shape=(
             jax.ShapeDtypeStruct((units, slots), BF16),
             jax.ShapeDtypeStruct((units, width), BF16),
-            jax.ShapeDtypeStruct((8, TOK), F32),
+            jax.ShapeDtypeStruct((TOP, TOK), F32),
         ),
-        in_specs=[vmem, vmem, anywhere, anywhere, anywhere],
+        in_specs=[hbm] * 5,
         out_specs=(anywhere, anywhere, vmem),
         scratch_shapes=[
+            pltpu.VMEM((TOP, TOK), jnp.int32),
+            pltpu.VMEM((TOP, TOK), BF16),
             pltpu.VMEM((NE * TOK, width), BF16),
             pltpu.VMEM((units, width), BF16),
             pltpu.VMEM((units, slots), BF16),
@@ -299,25 +358,29 @@
             pltpu.VMEM((NX, 2, 8, 128), F32),
             pltpu.VMEM((NE, 8, 128), F32),
             pltpu.VMEM((PLANE, 8, 128), F32),
-            dma((3,)),
+            dma((5,)),
             dma((2,)),
             dma((28,)),
             dma((8, 4)),
             dma((8, 4)),
             dma((8, 4)),
-            dma((NE,)),
-            dma((NE,)),
+            dma((7,)),
+            dma((8,)),
+            dma((8,)),
+            dma((8,)),
             dma((NE,)),
             dma((NE,)),
             dma((PLANE,)),
             dma((PLANE,)),
+            pltpu.SemaphoreType.REGULAR((5,)),
+            pltpu.SemaphoreType.REGULAR,
         ],
         compiler_params=pltpu.CompilerParams(collective_id=0, has_side_effects=True, vmem_limit_bytes=40 * 2**20),
         cost_estimate=pl.CostEstimate(
             flops=4 * units * width * NE * TOK, bytes_accessed=4 * units * width, transcendentals=0
         ),
-    )(expert_ids, gate_probs, grad_out, hidden, weight)
-    return gh[None], gd[None], scores[:TOP].T
+    )(*(pltpu.with_memory_space_constraint(a, pltpu.HBM) for a in (expert_ids.T, gate_probs.T, grad_out, hidden, weight)))
+    return gh[None], gd[None], scores.T
 
 
 def solution(mesh):

time: 65.6 us -> 53.3 us (0.81)
  Pallas kernels: 57.9 us -> 50.3 us
  local copies, waits for them, and re-layouts: 6.79 us -> 2.21 us
    pallas_call x1, Pallas kernels: 57.9 us -> 50.3 us  [shards(): pl.pallas_call(kernel, out_shape=(jax.ShapeDtypeStruct((units, slots), BF...]
    unnamed x14 -> x3, local copies, waits for them, and re-layouts: 6.21 us -> 2.21 us
where the time goes in v2:
time: 53.3 us; the launch traced here: 53.1 us
  Pallas kernels  50.3 us (94%)
  local copies, waits for them, and re-layouts  2.21 us (4%)
  between operations  0.64 us (1%)
    pallas_call x1, Pallas kernels, shards(): pl.pallas_call(kernel, out_shape=(jax.ShapeDtypeStruct((units, slots), BF...  50.3 us
    unnamed x3, local copies, waits for them, and re-layouts  2.21 us

profile of v2, /device:TPU:1, one launch (start us, length us, event | category | flops | bytes accessed | tf_op | source)
XLA Modules:
  0.0 53.1 jit_solution(11456233649520027760)
XLA Ops:
  0.6 50.3 %shard_map.76 = (bf16[168,512]{1,0:T(8,128)(2,1)S(1)}, bf16[168,3072]{1,0:T(8,128)(2,1)S(1)}, f32[4,64]{1,0:T(4,128)S(1)}) custom-call(s32[4,64]{1,0:T(4,128)} %bitcast.12, bf16[4,64]{1,0:T(4,128)(2,1)} %bitcast.13, bf16[64,3072]{1,0:T(8,128)(2,1)} %tok_hbm.1, bf16[168,512]{1,0:T(8,128)(2,1)} %bitcast.11, bf16[168,3072]{1,0:T(8,128)(2,1)} %bitcast.10), custom_call_target="tpu_custom_call" | custom-call | flops 2113929216 | bytes 2064384 | tf_op jit(solution)/shard_map/pallas_call | solution.py:338
  50.9 0.7 %copy.11 = bf16[1,168,512]{2,1,0:T(8,128)(2,1)} copy(bf16[1,168,512]{2,1,0:T(8,128)(2,1)S(1)} %bitcast.8) | data formatting | bytes 344064
  51.6 1.0 %copy.12 = bf16[1,168,3072]{2,1,0:T(8,128)(2,1)} copy(bf16[1,168,3072]{2,1,0:T(8,128)(2,1)S(1)} %bitcast.7) | data formatting | bytes 2064384
  52.6 0.6 %copy.13 = f32[64,4]{0,1:T(4,128)} copy(f32[64,4]{0,1:T(4,128)S(1)} %bitcast.9) | data formatting | bytes 2048

commit v3 on v2

v3 whole, which is shorter than its diff:
```python
import functools

import jax
import jax.numpy as jnp
from jax import lax
from jax.experimental import pallas as pl
from jax.experimental.pallas import tpu as pltpu
from jax.sharding import PartitionSpec as P

MESH = pl.DeviceIdType.MESH
NX, NY, NR = 4, 8, 4
NE = 16
TOK, TOP, CAP = 64, 4, 32
CH = 16
STRIPS = 2
PLANE = NY * NR
F32, BF16 = jnp.float32, jnp.bfloat16


def kernel(
    ids_hbm, gates_hbm, tok_hbm, hid_hbm, w_hbm,
    gh_hbm, gd_hbm, score_hbm,
    scores, ids, gates, rows, w, hid, spread, hs, scaled, pick, mine, gate, gh, gd, before, meta, part, sc1, sc2,
    load_sem, out_sem, ss, rs, rb, ds, rd, ms, mr, mds, mdr, s1_s, s1_r, s2_s, s2_r, wave, ready,
):
    e, y, r = lax.axis_index("expert"), lax.axis_index("shard"), lax.axis_index("replica")
    x, half, core = e // 4, (e // 2) % 2, e % 2
    plane = y * NR + r
    cls = (y + 2 * r) % 4

    def expert(xx, hh, cc):
        return xx * 4 + hh * 2 + cc

    def block(xx, hh, cc):
        return hh * 8 + xx * 2 + cc

    own = block(x, half, core)
    x1 = (expert((x + 1) % NX, half, core), y, r)
    x3 = (expert((x + 3) % NX, half, core), y, r)
    x2 = (expert((x + 2) % NX, half, core), y, r)
    y1, y7 = (e, (y + 1) % NY, r), (e, (y + 7) % NY, r)
    zn = (e, y, r + 1 - 2 * (r % 2))
    far = (e, y, (r + 2) % NR)
    mirror = (expert(x, 1 - half, core), y, NR - 1 - r)
    twin = (expert(x, half, 1 - core), y, r)

    barrier = pltpu.get_barrier_semaphore()
    near = (x1, x3, x2, y1, y7, zn, far, twin)
    for other in near:
        pl.semaphore_signal(barrier, inc=1, device_id=other, device_id_type=MESH)

    @pl.when(half == 0)
    def _():
        pl.semaphore_signal(barrier, inc=1, device_id=mirror, device_id_type=MESH)

    own_row = pl.multiple_of(own * TOK, TOK)
    load_tok = pltpu.make_async_copy(tok_hbm, rows.at[pl.ds(own_row, TOK)], load_sem.at[0])
    load_w = pltpu.make_async_copy(w_hbm, w, load_sem.at[1])
    load_h = pltpu.make_async_copy(hid_hbm, hid, load_sem.at[2])
    load_ids = pltpu.make_async_copy(ids_hbm, ids, load_sem.at[3])
    load_gates = pltpu.make_async_copy(gates_hbm, gates, load_sem.at[4])
    load_tok.start()
    load_ids.start()
    load_gates.start()
    load_w.start()
    load_h.start()

    place = (
        lax.broadcasted_iota(jnp.int32, (TOK, 128), 1)
        == lax.broadcasted_iota(jnp.int32, (TOK, 128), 0) + TOK * core
    ).astype(F32).astype(BF16)
    load_ids.wait()
    load_gates.wait()
    meta[own, 0:4, :] = jnp.dot(ids[...].astype(F32).astype(BF16), place, preferred_element_type=F32)
    meta[own, 4:8, :] = jnp.dot(gates[...], place, preferred_element_type=F32)
    pl.semaphore_wait(barrier, len(near) + half)

    @pl.when(half == 1)
    def _():
        pl.semaphore_signal(ready, inc=1, device_id=mirror, device_id_type=MESH)

    def ripple(n, *others):
        for other in others:
            pl.semaphore_signal(wave.at[n], inc=1, device_id=other, device_id_type=MESH)

    ripple(0, y1, y7)

    sent, shared = [], []

    def block_row(h, dx, cc, k):
        b = block((x + dx) % NX, half if h == 0 else 1 - half, cc)
        return pl.multiple_of(b * TOK + k * CH, CH)

    wide = rows.shape[1]
    whole = pl.ds(0, wide)
    strips = [pl.ds(n * (wide // STRIPS), wide // STRIPS) for n in range(STRIPS)]

    def arrival(h, dx, k, n=None):
        ref = rows.at[pl.ds(block_row(h, dx, core, k), CH), whole if n is None else strips[n]]
        sem = rs.at[h * 4 + dx, k] if n is None else rb.at[dx, n]
        return pltpu.make_async_remote_copy(
            src_ref=ref, dst_ref=ref, send_sem=ss, recv_sem=sem, device_id=x1, device_id_type=MESH
        )

    def from_twin(h, dx):
        ref = rows.at[pl.ds(block_row(h, dx, 1 - core, 0), TOK)]
        pltpu.make_async_remote_copy(
            src_ref=ref, dst_ref=ref, send_sem=ss, recv_sem=rd.at[h * 4 + dx], device_id=twin, device_id_type=MESH
        ).wait_recv()

    def outgoing(h, dx, k, to, there_h, there_dx, n=None, first=False):
        ref = rows.at[pl.ds(block_row(h, dx, core, k), CH), whole if n is None else strips[n]]
        sem = rb.at[there_dx, n] if first else rs.at[there_h * 4 + there_dx, k]
        copy = pltpu.make_async_remote_copy(
            src_ref=ref, dst_ref=ref, send_sem=ss, recv_sem=sem, device_id=to, device_id_type=MESH
        )
        sent.append(CH if n is None else CH / STRIPS)
        return copy

    def send(*what, **how):
        outgoing(*what, **how).start()

    def share(h, dx, k, count=1):
        ref = rows.at[pl.ds(block_row(h, dx, core, k), CH * count)]
        copy = pltpu.make_async_remote_copy(
            src_ref=ref, dst_ref=ref, send_sem=ds, recv_sem=rd.at[h * 4 + dx],
            device_id=twin, device_id_type=MESH,
        )
        copy.start()
        shared.append(CH * count)

    def meta_copy(h, dx, to, send_sem, recv_sem, cc):
        ref = meta.at[block((x + dx) % NX, half if h == 0 else 1 - half, cc)]
        return pltpu.make_async_remote_copy(
            src_ref=ref, dst_ref=ref, send_sem=send_sem, recv_sem=recv_sem, device_id=to, device_id_type=MESH
        )

    noted = []

    def note(h, dx, to, there_h, there_dx):
        copy = meta_copy(h, dx, to, ms, mr.at[there_h * 4 + there_dx], core)
        copy.start()
        noted.append(copy)

    def note_twin(h, dx):
        meta_copy(h, dx, twin, mds, mdr, core).start()

    def noted_here(h, dx):
        meta_copy(h, dx, twin, ms, mr.at[h * 4 + dx], core).wait_recv()
        note_twin(h, dx)

    def all_of(ref, count, send_sem, recv_sem):
        some = ref.at[pl.ds(0, count)]
        return pltpu.make_async_remote_copy(
            src_ref=some, dst_ref=some, send_sem=send_sem, recv_sem=recv_sem, device_id=twin, device_id_type=MESH
        )

    def prepare():
        all_of(meta, 8, mds, mdr).wait_recv()
        named = jnp.concatenate([meta[2 * n] + meta[2 * n + 1] for n in range(NE // 2)], axis=1)
        is_mine = (named[0:4] == e.astype(F32)).astype(F32)
        took = jnp.sum(is_mine, axis=0, keepdims=True)
        its_gate = jnp.sum(is_mine * named[4:8], axis=0, keepdims=True)
        groups = [slice(256 * g, 256 * g + 256) for g in range(NX)]
        by_group = jnp.concatenate([took[:, here] for here in groups] + [jnp.zeros((4, 256), F32)], axis=0)
        position = jnp.dot(by_group.astype(BF16), before[...], preferred_element_type=F32)
        lane, line = (lax.broadcasted_iota(jnp.int32, (8, 256), d) for d in (1, 0))
        first_slot = lane // 128 * 128 + line // 2 * 64 + lane // TOK % 2 * CAP
        slot = jnp.where(by_group > 0.5, position.astype(jnp.int32) + first_slot, -1)
        slot_row = lax.broadcasted_iota(jnp.int32, (256, 256), 0)
        picked = [(slot_row == slot[g : g + 1]).astype(F32).astype(BF16) for g in range(NX)]
        of_tokens = [
            jnp.dot(hid[:, 256 * (g % 2) : 256 * (g % 2) + 256], picked[g], preferred_element_type=F32)
            for g in range(NX)
        ]
        mine[...] = jnp.concatenate([is_mine, jnp.zeros((4, NE * TOK), F32)], axis=0)
        gate[...] = jnp.broadcast_to(its_gate, (8, NE * TOK))
        for g, here in enumerate(groups):
            pick[g] = picked[g]
            hs[:, here] = of_tokens[g].astype(BF16)
            spread[:, here] = (of_tokens[g] * its_gate[:, here]).astype(BF16)

    k0, k1, k2, k3 = cls, (cls + 1) % 4, (cls + 2) % 4, (cls + 3) % 4
    along = ((x1, 3), (x3, 1), (x2, 2))

    load_tok.wait()
    for to, dx in along:
        note(0, 0, to, 0, dx)
        send(0, 0, k0, to, 0, dx)
    crossing = [meta_copy(0, 0, mirror, ms, mr.at[4], core)]
    noted.append(crossing[0])
    crossing += [outgoing(0, 0, k2, mirror, 1, 0, n, first=True) for n in range(STRIPS)]

    @pl.when(half == 0)
    def _():
        pl.semaphore_wait(ready, 1)

    for copy in crossing:
        copy.start()
    note_twin(0, 0)
    share(0, 0, 0, 4)
    send(0, 0, k2, x1, 0, 3)
    send(0, 0, k2, x3, 0, 1)

    t_from = lax.broadcasted_iota(jnp.int32, (256, 256), 0)
    t_to = lax.broadcasted_iota(jnp.int32, (256, 256), 1)
    before[...] = ((t_from < t_to) & (t_from // TOK == t_to // TOK)).astype(F32).astype(BF16)

    arrival(0, 2, k0).wait_recv()
    for to in (y1, y7, zn):
        send(0, 2, k0, to, 0, 2)
    share(0, 2, k0)
    for dx in (1, 3, 2):
        noted_here(0, dx)
    pl.semaphore_wait(wave.at[0], 2)
    ripple(1, y1, y7)

    noted_here(1, 0)
    for to, dx in along:
        note(1, 0, to, 1, dx)
    for n in range(STRIPS):
        arrival(1, 0, k0, n).wait_recv()
        for to, dx in along:
            send(1, 0, k0, to, 1, dx, n, first=True)
        for to in (y1, y7, zn):
            send(1, 0, k0, to, 1, 0, n)
    for kk in (k1, k3):
        send(0, 0, kk, x1, 0, 3)
        send(0, 0, kk, x3, 0, 1)
    share(1, 0, k0)
    for dx in (1, 3, 2):
        noted_here(1, dx)
    pl.semaphore_wait(wave.at[1], 2)
    ripple(2, y1, y7)
    for dx in (1, 3):
        arrival(0, dx, k0).wait_recv()
        share(0, dx, k0)
    for n in range(STRIPS):
        for dx in (1, 3, 2):
            arrival(1, dx, k0, n).wait_recv()
            for to in (y1, y7, zn):
                send(1, dx, k0, to, 1, dx, n)
    for dx in (1, 3, 2):
        share(1, dx, k0)
    pl.semaphore_wait(wave.at[2], 2)
    ripple(3, zn)

    load_h.wait()
    prepare()
    load_w.wait()

    def bring(h, dx):
        for k in (k2, k1, k3):
            arrival(h, dx, k).wait_recv()
            share(h, dx, k)

    by_row = (((1,), (1,)), ((), ()))
    scored = []

    def multiply(i):
        hh = half if i == 0 else 1 - half
        for dx in range(NX):
            if (i, dx) != (0, 0):
                from_twin(i, dx)
        here = pl.ds(pl.multiple_of(hh * 512, 512), 512)
        proj = lax.dot_general(w[...], rows[here, :], by_row, preferred_element_type=F32)
        terms = mine[:, here] * jnp.sum(hs[:, here].astype(F32) * proj, axis=0, keepdims=True)
        for n in range(NX):
            part[i, n] = terms[:, 128 * n : 128 * n + 128]
        for dx in (2, 1, 3, 0):
            xx = (x + dx) % NX
            for cc in range(2):
                if (i, dx, cc) == (0, 0, 0):
                    continue
                copy = pltpu.make_async_remote_copy(
                    src_ref=part.at[i, xx], dst_ref=sc1.at[e], send_sem=s1_s, recv_sem=s1_r,
                    device_id=(expert(xx, hh, core if cc == 0 else 1 - core), y, r if i == 0 else NR - 1 - r),
                    device_id_type=MESH,
                )
                copy.start()
                scored.append(copy)
        if i == 0:
            sc1[e] = part[0, x]
        scaled[:, here] = (proj * gate[0:1, here]).astype(BF16)

    for dx in (2, 1, 3):
        bring(0, dx)
    bring(1, 0)
    pl.semaphore_wait(wave.at[3], 1)
    ripple(4, far)
    from_twin(0, 0)
    multiply(0)
    for dx in (1, 3, 2):
        bring(1, dx)
    multiply(1)

    for n in range(2):
        slots = slice(256 * n, 256 * n + 256)
        gh[:, slots] = sum(
            lax.dot_general(scaled[:, 256 * g : 256 * g + 256], pick[g], by_row, preferred_element_type=F32)
            for g in (n, n + 2)
        ).astype(BF16)

    out_h = pltpu.make_async_copy(gh, gh_hbm, out_sem.at[0])
    out_h.start()

    width = 512

    def weight_columns(first, last):
        for j in range(first, last):
            cols = pl.ds(j * width, width)
            gd[:, cols] = jnp.dot(spread[...], rows[:, cols], preferred_element_type=F32).astype(BF16)

    weight_columns(0, 3)

    all_of(sc1, NE - 1, s1_s, s1_r).wait_recv()
    sc2[plane] = jnp.sum(sc1[...], axis=0)

    def tell(k, _):
        p = (plane + k) % PLANE
        pltpu.make_async_remote_copy(
            src_ref=sc2.at[plane], dst_ref=sc2.at[plane], send_sem=s2_s, recv_sem=s2_r,
            device_id=(e, p // NR, p % NR), device_id_type=MESH,
        ).start()
        return 0

    pl.semaphore_wait(wave.at[4], 1)
    lax.fori_loop(1, PLANE, tell, 0)

    weight_columns(3, gd.shape[1] // width)
    out_d = pltpu.make_async_copy(gd, gd_hbm, out_sem.at[1])
    out_d.start()

    assert len(noted) == 7 and len(scored) == NE - 1
    all_of(rows, int(sum(sent)), ss, ss).wait_send()
    all_of(rows, sum(shared), ds, ds).wait_send()
    all_of(meta, len(noted), ms, ms).wait_send()
    all_of(meta, 8, mds, mds).wait_send()
    all_of(sc1, len(scored), s1_s, s1_s).wait_send()
    out_h.wait()
    out_d.wait()
    exchange = all_of(sc2, PLANE - 1, s2_s, s2_r)
    exchange.wait_recv()
    total = jnp.sum(sc2[...], axis=0)
    scores[...] = jnp.where(core == 0, total[0:TOP, 0:TOK], total[0:TOP, TOK : 2 * TOK])
    out_s = pltpu.make_async_copy(scores, score_hbm, out_sem.at[2])
    out_s.start()
    exchange.wait_send()
    out_s.wait()


def shards(grad_out, gate_probs, expert_ids, saved_hidden, down_weight):
    hidden, weight = saved_hidden[0], down_weight[0]
    units, slots = hidden.shape
    width = weight.shape[1]
    dma = pltpu.SemaphoreType.DMA
    anywhere = pl.BlockSpec(memory_space=pl.ANY)
    hbm = pl.BlockSpec(memory_space=pltpu.HBM)
    gh, gd, scores = pl.pallas_call(
        kernel,
        out_shape=(
            jax.ShapeDtypeStruct((units, slots), BF16),
            jax.ShapeDtypeStruct((units, width), BF16),
            jax.ShapeDtypeStruct((TOP, TOK), F32),
        ),
        in_specs=[hbm] * 5,
        out_specs=(anywhere,) * 3,
        scratch_shapes=[
            pltpu.VMEM((TOP, TOK), F32),
            pltpu.VMEM((TOP, TOK), jnp.int32),
            pltpu.VMEM((TOP, TOK), BF16),
            pltpu.VMEM((NE * TOK, width), BF16),
            pltpu.VMEM((units, width), BF16),
            pltpu.VMEM((units, slots), BF16),
            pltpu.VMEM((units, NE * TOK), BF16),
            pltpu.VMEM((units, NE * TOK), BF16),
            pltpu.VMEM((units, NE * TOK), BF16),
            pltpu.VMEM((NX, 256, 256), BF16),
            pltpu.VMEM((8, NE * TOK), F32),
            pltpu.VMEM((8, NE * TOK), F32),
            pltpu.VMEM((units, slots), BF16),
            pltpu.VMEM((units, width), BF16),
            pltpu.VMEM((256, 256), BF16),
            pltpu.VMEM((NE, 8, 128), F32),
            pltpu.VMEM((2, NX, 8, 128), F32),
            pltpu.VMEM((NE, 8, 128), F32),
            pltpu.VMEM((PLANE, 8, 128), F32),
            dma((5,)),
            dma((3,)),
            dma,
            dma((8, 4)),
            dma((NX, STRIPS)),
            dma,
            dma((8,)),
            dma,
            dma((8,)),
            dma,
            dma,
            dma,
            dma,
            dma,
            dma,
            pltpu.SemaphoreType.REGULAR((5,)),
            pltpu.SemaphoreType.REGULAR,
        ],
        compiler_params=pltpu.CompilerParams(collective_id=0, has_side_effects=True, vmem_limit_bytes=40 * 2**20),
        cost_estimate=pl.CostEstimate(
            flops=4 * units * width * NE * TOK, bytes_accessed=4 * units * width, transcendentals=0
        ),
    )(*(pltpu.with_memory_space_constraint(a, pltpu.HBM) for a in (expert_ids.T, gate_probs.T, grad_out, hidden, weight)))
    return gh[None], gd[None], scores.T


def solution(mesh):
    split = P("expert", ("shard", "replica"), None)
    rows = P("expert", None)
    return jax.shard_map(
        shards, mesh=mesh, in_specs=(rows, rows, rows, split, split), out_specs=(split, split, rows), check_vma=False
    )
```

time: 53.3 us -> 52.4 us (0.983)
  Pallas kernels: 50.3 us -> 49.4 us
    pallas_call x1, Pallas kernels: 50.3 us -> 49.4 us  [shards(): pl.pallas_call(kernel, out_shape=(jax.ShapeDtypeStruct((units, slots), BF...]
where the time goes in v3:
time: 52.4 us; the launch traced here: 52.3 us
  Pallas kernels  49.4 us (94%)
  local copies, waits for them, and re-layouts  2.21 us (4%)
  between operations  0.64 us (1%)
    pallas_call x1, Pallas kernels, shards(): pl.pallas_call(kernel, out_shape=(jax.ShapeDtypeStruct((units, slots), BF...  49.4 us
    unnamed x3, local copies, waits for them, and re-layouts  2.21 us

profile of v3, /device:TPU:1, one launch (start us, length us, event | category | flops | bytes accessed | tf_op | source)
XLA Modules:
  0.0 52.3 jit_solution(6676620319179774246)
XLA Ops:
  0.6 49.4 %shard_map.76 = (bf16[168,512]{1,0:T(8,128)(2,1)S(1)}, bf16[168,3072]{1,0:T(8,128)(2,1)S(1)}, f32[4,64]{1,0:T(4,128)S(1)}) custom-call(s32[4,64]{1,0:T(4,128)} %bitcast.12, bf16[4,64]{1,0:T(4,128)(2,1)} %bitcast.13, bf16[64,3072]{1,0:T(8,128)(2,1)} %tok_hbm.1, bf16[168,512]{1,0:T(8,128)(2,1)} %bitcast.11, bf16[168,3072]{1,0:T(8,128)(2,1)} %bitcast.10), custom_call_target="tpu_custom_call" | custom-call | flops 2113929216 | bytes 2064384 | tf_op jit(solution)/shard_map/pallas_call | solution.py:359
  50.1 0.7 %copy.11 = bf16[1,168,512]{2,1,0:T(8,128)(2,1)} copy(bf16[1,168,512]{2,1,0:T(8,128)(2,1)S(1)} %bitcast.8) | data formatting | bytes 344064
  50.7 1.0 %copy.12 = bf16[1,168,3072]{2,1,0:T(8,128)(2,1)} copy(bf16[1,168,3072]{2,1,0:T(8,128)(2,1)S(1)} %bitcast.7) | data formatting | bytes 2064384
  51.7 0.6 %copy.13 = f32[64,4]{0,1:T(4,128)} copy(f32[64,4]{0,1:T(4,128)S(1)} %bitcast.9) | data formatting | bytes 2048

commit v4 on v3

--- a/solution.py
+++ b/solution.py
@@ -255,7 +255,6 @@
             share(h, dx, k)
 
     by_row = (((1,), (1,)), ((), ()))
-    scored = []
 
     def multiply(i):
         hh = half if i == 0 else 1 - half
@@ -272,13 +271,11 @@
             for cc in range(2):
                 if (i, dx, cc) == (0, 0, 0):
                     continue
-                copy = pltpu.make_async_remote_copy(
+                pltpu.make_async_remote_copy(
                     src_ref=part.at[i, xx], dst_ref=sc1.at[e], send_sem=s1_s, recv_sem=s1_r,
                     device_id=(expert(xx, hh, core if cc == 0 else 1 - core), y, r if i == 0 else NR - 1 - r),
                     device_id_type=MESH,
-                )
-                copy.start()
-                scored.append(copy)
+                ).start()
         if i == 0:
             sc1[e] = part[0, x]
         scaled[:, here] = (proj * gate[0:1, here]).astype(BF16)
@@ -289,9 +286,18 @@
     pl.semaphore_wait(wave.at[3], 1)
     ripple(4, far)
     from_twin(0, 0)
-    multiply(0)
+
+    @pl.when(core == 0)
+    def _():
+        multiply(0)
+
     for dx in (1, 3, 2):
         bring(1, dx)
+
+    @pl.when(core == 1)
+    def _():
+        multiply(0)
+
     multiply(1)
 
     for n in range(2):
@@ -316,8 +322,8 @@
     all_of(sc1, NE - 1, s1_s, s1_r).wait_recv()
     sc2[plane] = jnp.sum(sc1[...], axis=0)
 
-    def tell(k, _):
-        p = (plane + k) % PLANE
+    def tell(n, _):
+        p = (plane + PLANE // 2 + (n + 1) // 2 * (1 - 2 * (n % 2))) % PLANE
         pltpu.make_async_remote_copy(
             src_ref=sc2.at[plane], dst_ref=sc2.at[plane], send_sem=s2_s, recv_sem=s2_r,
             device_id=(e, p // NR, p % NR), device_id_type=MESH,
@@ -325,18 +331,18 @@
         return 0
 
     pl.semaphore_wait(wave.at[4], 1)
-    lax.fori_loop(1, PLANE, tell, 0)
+    lax.fori_loop(0, PLANE - 1, tell, 0)
 
     weight_columns(3, gd.shape[1] // width)
     out_d = pltpu.make_async_copy(gd, gd_hbm, out_sem.at[1])
     out_d.start()
 
-    assert len(noted) == 7 and len(scored) == NE - 1
+    assert len(noted) == 7
     all_of(rows, int(sum(sent)), ss, ss).wait_send()
     all_of(rows, sum(shared), ds, ds).wait_send()
     all_of(meta, len(noted), ms, ms).wait_send()
     all_of(meta, 8, mds, mds).wait_send()
-    all_of(sc1, len(scored), s1_s, s1_s).wait_send()
+    all_of(sc1, NE - 1, s1_s, s1_s).wait_send()
     out_h.wait()
     out_d.wait()
     exchange = all_of(sc2, PLANE - 1, s2_s, s2_r)

time: 52.4 us -> 49.9 us (0.952)
  Pallas kernels: 49.4 us -> 46.9 us
    pallas_call x1, Pallas kernels: 49.4 us -> 46.9 us  [shards(): pl.pallas_call(kernel, out_shape=(jax.ShapeDtypeStruct((units, slots), BF...]
where the time goes in v4:
time: 49.9 us; the launch traced here: 49.8 us
  Pallas kernels  46.9 us (94%)
  local copies, waits for them, and re-layouts  2.21 us (4%)
  between operations  0.64 us (1%)
    pallas_call x1, Pallas kernels, shards(): pl.pallas_call(kernel, out_shape=(jax.ShapeDtypeStruct((units, slots), BF...  46.9 us
    unnamed x3, local copies, waits for them, and re-layouts  2.21 us

profile of v4, /device:TPU:1, one launch (start us, length us, event | category | flops | bytes accessed | tf_op | source)
XLA Modules:
  0.0 49.8 jit_solution(18023643287945997183)
XLA Ops:
  0.6 46.9 %shard_map.76 = (bf16[168,512]{1,0:T(8,128)(2,1)S(1)}, bf16[168,3072]{1,0:T(8,128)(2,1)S(1)}, f32[4,64]{1,0:T(4,128)S(1)}) custom-call(s32[4,64]{1,0:T(4,128)} %bitcast.12, bf16[4,64]{1,0:T(4,128)(2,1)} %bitcast.13, bf16[64,3072]{1,0:T(8,128)(2,1)} %tok_hbm.1, bf16[168,512]{1,0:T(8,128)(2,1)} %bitcast.11, bf16[168,3072]{1,0:T(8,128)(2,1)} %bitcast.10), custom_call_target="tpu_custom_call" | custom-call | flops 2113929216 | bytes 2064384 | tf_op jit(solution)/shard_map/pallas_call | solution.py:365
  47.5 0.7 %copy.11 = bf16[1,168,512]{2,1,0:T(8,128)(2,1)} copy(bf16[1,168,512]{2,1,0:T(8,128)(2,1)S(1)} %bitcast.8) | data formatting | bytes 344064
  48.2 1.0 %copy.12 = bf16[1,168,3072]{2,1,0:T(8,128)(2,1)} copy(bf16[1,168,3072]{2,1,0:T(8,128)(2,1)S(1)} %bitcast.7) | data formatting | bytes 2064384
  49.2 0.6 %copy.13 = f32[64,4]{0,1:T(4,128)} copy(f32[64,4]{0,1:T(4,128)S(1)} %bitcast.9) | data formatting | bytes 2048

commit v5 on v4

--- a/solution.py
+++ b/solution.py
@@ -184,19 +184,25 @@
     along = ((x1, 3), (x3, 1), (x2, 2))
 
     load_tok.wait()
+    crossing = [meta_copy(0, 0, mirror, ms, mr.at[4], core)]
+    noted.append(crossing[0])
+    crossing += [outgoing(0, 0, k2, mirror, 1, 0, n, first=True) for n in range(STRIPS)]
+
+    @pl.when(half == 1)
+    def _():
+        for copy in crossing:
+            copy.start()
+
     for to, dx in along:
         note(0, 0, to, 0, dx)
         send(0, 0, k0, to, 0, dx)
-    crossing = [meta_copy(0, 0, mirror, ms, mr.at[4], core)]
-    noted.append(crossing[0])
-    crossing += [outgoing(0, 0, k2, mirror, 1, 0, n, first=True) for n in range(STRIPS)]
 
     @pl.when(half == 0)
     def _():
         pl.semaphore_wait(ready, 1)
-
-    for copy in crossing:
-        copy.start()
+        for copy in crossing:
+            copy.start()
+
     note_twin(0, 0)
     share(0, 0, 0, 4)
     send(0, 0, k2, x1, 0, 3)

time: 49.9 us -> 49.9 us (level)
  no operation moved by 1% of the time
where the time goes in v5:
time: 49.9 us; the launch traced here: 49.8 us
  Pallas kernels  46.9 us (94%)
  local copies, waits for them, and re-layouts  2.21 us (4%)
  between operations  0.64 us (1%)
    pallas_call x1, Pallas kernels, shards(): pl.pallas_call(kernel, out_shape=(jax.ShapeDtypeStruct((units, slots), BF...  46.9 us
    unnamed x3, local copies, waits for them, and re-layouts  2.21 us

profile of v5, /device:TPU:1, one launch (start us, length us, event | category | flops | bytes accessed | tf_op | source)
XLA Modules:
  0.0 49.8 jit_solution(17030894579983617414)
XLA Ops:
  0.6 46.9 %shard_map.76 = (bf16[168,512]{1,0:T(8,128)(2,1)S(1)}, bf16[168,3072]{1,0:T(8,128)(2,1)S(1)}, f32[4,64]{1,0:T(4,128)S(1)}) custom-call(s32[4,64]{1,0:T(4,128)} %bitcast.12, bf16[4,64]{1,0:T(4,128)(2,1)} %bitcast.13, bf16[64,3072]{1,0:T(8,128)(2,1)} %tok_hbm.1, bf16[168,512]{1,0:T(8,128)(2,1)} %bitcast.11, bf16[168,3072]{1,0:T(8,128)(2,1)} %bitcast.10), custom_call_target="tpu_custom_call" | custom-call | flops 2113929216 | bytes 2064384 | tf_op jit(solution)/shard_map/pallas_call | solution.py:371
  47.5 0.7 %copy.11 = bf16[1,168,512]{2,1,0:T(8,128)(2,1)} copy(bf16[1,168,512]{2,1,0:T(8,128)(2,1)S(1)} %bitcast.8) | data formatting | bytes 344064
  48.2 1.0 %copy.12 = bf16[1,168,3072]{2,1,0:T(8,128)(2,1)} copy(bf16[1,168,3072]{2,1,0:T(8,128)(2,1)S(1)} %bitcast.7) | data formatting | bytes 2064384
  49.2 0.6 %copy.13 = f32[64,4]{0,1:T(4,128)} copy(f32[64,4]{0,1:T(4,128)S(1)} %bitcast.9) | data formatting | bytes 2048
